TPU v7x, 32 devices: a whole 2x2x4 slice. The times are simulated.
32 devices in a mesh: cont: 4 (over z), line: 2 (over y), scen: 4 (over x, core).
Axes of the slice: x: 2, y: 2, z: 4, core: 2. Of those that a mesh axis runs over, the one named last changes fastest.
Arguments:
- lodf: bfloat16 [256, 4096], P('line', 'cont'), may hold values from -1 to 1
- flow: float32 [256, 256], P('line', 'scen'), may hold values from -6 to 6
- out_flow: float32 [256, 4096], P('scen', 'cont'), may hold values from -6 to 6
- limits: float32 [256], P('line'), may hold values from 0.5 to 2
- ptdf_mon: bfloat16 [256, 2048], P('line'), may hold values from -6 to 6
- ptdf_out: bfloat16 [4096, 2048], P('cont'), may hold values from -6 to 6
- viol_cont: int32 [16384], P(('cont', 'line', 'scen')), may hold values from 0 to 1023
- viol_line: int32 [16384], P(('cont', 'line', 'scen')), may hold values from 0 to 127
- viol_scen: int32 [16384], P(('cont', 'line', 'scen')), may hold values from 0 to 63
- rows_used: int32 [32], P(('cont', 'line', 'scen')), may hold values from 64 to 512, as said below
Outputs:
- worst: float32 [256, 256], P('line', 'scen')
- schur: float32 [2048, 2048], P(('line', 'scen'))
Inputs may be any that keep to these rules, and one draw needn't show every extreme that they name: `rows_used`: each device uses a leading run of its 512 slots; the counts are skewed, and some device is full.
All inputs are finite; a program needn't handle non-finite values.
Results may differ from a plain program's by a relative error of at most 0.00096.
Values may be sent and summed in bfloat16 or wider, within the bound.
A program may use at most 128 MiB of HBM per device.

v0:
```python
import functools
import math

import jax
import jax.numpy as jnp
from jax import lax
from jax.experimental import pallas as pl
from jax.experimental.pallas import tpu as pltpu
from jax.sharding import PartitionSpec as P


MESH = pl.DeviceIdType.MESH
F32 = jnp.float32
BF16 = jnp.bfloat16
CODE = 32760.0


def encode(x):
    top = jnp.maximum(jnp.max(jnp.abs(x), axis=0, keepdims=True), 1e-30)
    unit = x * (1.0 / top)
    root = unit * lax.rsqrt(jnp.maximum(jnp.abs(unit), 1e-30)) * CODE
    code = jnp.round(root).astype(jnp.int32).astype(jnp.int16)
    return code, jnp.broadcast_to(top * (1.0 / (CODE * CODE)), (8, x.shape[1]))


def decode(code, unit):
    root = code.astype(jnp.int32).astype(F32)
    return root * jnp.abs(root) * unit[0:1, :]


def kernel(
    dims, line_ref, cont_ref, scen_ref, used_ref, lim_ref, lodf_ref, flow_t, out_flow_ref, mon_ref, out_ref,
    worst_ref, code_ref, unit_ref,
    meta, lodf32, high, low, loading, pick, weight, left, scaled, own,
    q_send, q_recv, u_send, u_recv, meta_ss, meta_rs, load_ss, load_rs, send_sems, recv_sems,
):
    n_cont, n_line, n_scen = dims
    c, m, q = lax.axis_index("cont"), lax.axis_index("line"), lax.axis_index("scen")
    pair = c + 1 - 2 * lax.rem(c, 2)
    middle = n_cont - 1 - c
    outer = jnp.logical_or(c == 0, c == n_cont - 1)
    inner = jnp.logical_not(outer)
    other = 1 - m
    n_rows = line_ref.shape[1]
    lines, width = mon_ref.shape
    conts = out_ref.shape[0]
    scens = flow_t.shape[0]
    block = code_ref.shape[0]
    chunks = width // block
    half = block // 2
    items = 2 * chunks
    parts = n_rows // 128

    barrier = pltpu.get_barrier_semaphore()
    for d in range(1, n_scen):
        pl.semaphore_signal(barrier, inc=1, device_id={"scen": lax.rem(q + d, n_scen)}, device_id_type=MESH)
    for d in range(1, n_cont):
        pl.semaphore_signal(barrier, inc=1, device_id={"cont": lax.rem(c + d, n_cont)}, device_id_type=MESH)
    pl.semaphore_signal(barrier, inc=1, device_id={"line": other}, device_id_type=MESH)

    meta[8 * n_scen:, :] = jnp.zeros((128 - 8 * n_scen, n_rows), F32)
    for p in range(parts):
        at = slice(p * 128, (p + 1) * 128)
        sub = lax.broadcasted_iota(jnp.int32, (128, 128), 0)
        cols = jnp.where(sub == 0, line_ref[:, at], jnp.where(sub == 1, cont_ref[:, at], jnp.where(sub == 2, scen_ref[:, at], used_ref[...])))
        cols = jnp.transpose(cols.astype(F32))
        v_line, v_cont, v_scen, used = cols[:, 0:1], cols[:, 1:2], cols[:, 2:3], cols[:, 3:4]
        lane = lax.broadcasted_iota(jnp.int32, (128, 128), 1)
        is_line = lax.broadcasted_iota(jnp.int32, (128, lines), 1).astype(F32) == v_line
        is_cont = lax.broadcasted_iota(jnp.int32, (128, conts), 1).astype(F32) == v_cont
        is_scen = lax.broadcasted_iota(jnp.int32, (128, scens), 1).astype(F32) == v_scen
        one_line, one_scen = is_line.astype(F32), is_scen.astype(F32)
        row = jnp.dot(one_line.astype(BF16), lodf_ref[...], preferred_element_type=F32)
        coef = jnp.sum(jnp.where(is_cont, row, 0.0), axis=1, keepdims=True)
        row = jnp.dot(one_scen, flow_t[...], precision=lax.Precision.HIGHEST, preferred_element_type=F32)
        base = jnp.sum(jnp.where(is_line, row, 0.0), axis=1, keepdims=True)
        row = jnp.dot(one_scen, out_flow_ref[...], precision=lax.Precision.HIGHEST, preferred_element_type=F32)
        outage = jnp.sum(jnp.where(is_cont, row, 0.0), axis=1, keepdims=True)
        limit = jnp.sum(jnp.where(is_line, lim_ref[...], 0.0), axis=1, keepdims=True)
        ratio = (base + coef * outage) / limit
        place = lax.broadcasted_iota(jnp.int32, (128, 1), 0).astype(F32) + float(p * 128)
        w = jnp.where(place < used, 1.0 + ratio * ratio, 0.0)
        facts = jnp.where(lane == 0, v_line, jnp.where(lane == 1, v_cont, jnp.where(lane == 2, coef, jnp.where(lane == 3, w, 0.0))))
        meta[pl.ds(pl.multiple_of(q * 8, 8), 8), at] = jnp.transpose(facts)[0:8, :]

    def meta_copy(source, target):
        rows = meta.at[pl.ds(pl.multiple_of(source * 8, 8), 8), :]
        return pltpu.make_async_remote_copy(
            src_ref=rows, dst_ref=rows, send_sem=meta_ss.at[target], recv_sem=meta_rs.at[source],
            device_id={"scen": target}, device_id_type=MESH)

    pl.semaphore_wait(barrier, n_scen + n_cont - 1)
    for d in range(1, n_scen):
        meta_copy(q, lax.rem(q + d, n_scen)).start()

    lodf32[...] = lodf_ref[...].astype(F32)
    high[...] = jnp.zeros_like(high)
    low[...] = jnp.zeros_like(low)

    for d in range(1, n_scen):
        source = lax.rem(q + d, n_scen)
        meta_copy(source, source).wait_recv()

    for s in range(n_scen):
        for p in range(parts):
            facts = jnp.transpose(meta[:, p * 128:(p + 1) * 128])
            f = facts[:, s * 8:(s + 1) * 8]
            at = slice(s * n_rows + p * 128, s * n_rows + (p + 1) * 128)
            lane = lax.broadcasted_iota(jnp.int32, (128, lines), 1).astype(F32)
            pick[at, 0:lines] = jnp.where(lane == f[:, 0:1], 1.0, 0.0).astype(BF16)
            lane = lax.broadcasted_iota(jnp.int32, (128, conts), 1).astype(F32)
            pick[at, lines:] = jnp.where(lane == f[:, 1:2], f[:, 2:3], 0.0).astype(BF16)
            weight[at, :] = jnp.broadcast_to(f[:, 3:4], (128, 128))

    def rows_of(s, column):
        at = pl.ds(pl.multiple_of(s * n_rows, n_rows), n_rows)
        cols = pl.ds(pl.multiple_of(column, block), block)
        full = jnp.dot(pick[at, 0:lines], mon_ref[:, cols], preferred_element_type=F32)
        full = full + jnp.dot(pick[at, lines:], out_ref[:, cols], preferred_element_type=F32)
        return full.astype(BF16)

    def screen(first, count):
        top, bottom = high[...], low[...]
        place = lax.broadcasted_iota(jnp.int32, (scens, lines), 1)
        for i in range(count):
            factors = lodf32[pl.ds(first + i, 1), :]
            tall = short = None
            for k in range(conts // 128):
                move = out_flow_ref[:, k * 128:(k + 1) * 128] * factors[:, k * 128:(k + 1) * 128]
                tall = move if tall is None else jnp.maximum(tall, move)
                short = move if short is None else jnp.minimum(short, move)
            top = jnp.where(place == first + i, jnp.max(tall, axis=1, keepdims=True), top)
            bottom = jnp.where(place == first + i, jnp.min(short, axis=1, keepdims=True), bottom)
        high[...] = top
        low[...] = bottom

    lines_each = lines // (chunks * n_scen)

    def scale(s, slot, rows):
        at = pl.ds(pl.multiple_of(s * n_rows, n_rows), n_rows)
        w = weight[at, :]
        w = jnp.concatenate([w] * (block // 128), axis=1)
        scaled[slot, at, :] = (rows.astype(F32) * w).astype(BF16)

    def column(t):
        return (lax.rem(t, n_line) * n_scen + lax.rem(q + t // n_line, n_scen)) * block

    def left_step(s, carry):
        at = pl.ds(pl.multiple_of(s * n_rows, n_rows), n_rows)
        for line in range(n_line):
            rows = rows_of(s, column(line))
            left[line * block:(line + 1) * block, at] = jnp.transpose(rows.astype(F32)).astype(BF16)
            scale(s, line, rows)
        screen(s * n_line * lines_each, n_line * lines_each)
        return carry

    lax.fori_loop(0, n_scen, left_step, 0)

    def link(stage, j, to):
        kinds = ((q_send, q_recv), (u_send, u_recv))
        return [
            pltpu.make_async_remote_copy(
                src_ref=a.at[stage, j], dst_ref=b.at[stage, j], send_sem=send_sems.at[kind, stage, j],
                recv_sem=recv_sems.at[kind, stage, j], device_id=to, device_id_type=MESH)
            for kind, (a, b) in enumerate(kinds)
        ]

    to_line, to_pair, to_middle = {"line": other}, {"cont": pair}, {"cont": middle}

    def send(stage, j, to, value):
        code, unit = encode(value)
        q_send[stage, j] = code
        u_send[stage, j] = unit
        for copy in link(stage, j, to):
            copy.start()

    def received(stage, j, to):
        for copy in link(stage, j, to):
            copy.wait_recv()
        return decode(q_recv[stage, j], u_recv[stage, j])

    def put(i, code, unit):
        at = pl.ds(pl.multiple_of(lax.rem(i, 2) * half, half), half)
        cols = pl.ds(pl.multiple_of(column(i // 2), block), block)
        code_ref[at, cols] = code
        unit_ref[pl.ds(pl.multiple_of(lax.rem(i, 2) * 8, 8), 8), cols] = unit

    def mine(i):
        return own.at[i // 2, pl.ds(pl.multiple_of(m * block + lax.rem(i, 2) * half, half), half), :]

    def load_copy(source, target):
        return pltpu.make_async_remote_copy(
            src_ref=loading.at[source], dst_ref=loading.at[source], send_sem=load_ss.at[target],
            recv_sem=load_rs.at[source], device_id={"cont": target}, device_id_type=MESH)

    def turn(u, carry):
        @pl.when(jnp.logical_and(lax.rem(u, 2) == 0, u < items))
        def _():
            t = u // 2
            slot = lax.rem(t, n_line)

            @pl.when(t >= n_line)
            def _():
                def scale_step(s, inside):
                    scale(s, slot, rows_of(s, column(t)))
                    screen((t * n_scen + s) * lines_each, lines_each)
                    return inside

                lax.fori_loop(0, n_scen, scale_step, 0)

            own[t] = jnp.dot(left[...], scaled[slot], preferred_element_type=F32)
            for h in range(2):
                send(0, u + h, to_line, own[t, pl.ds(pl.multiple_of(other * block + h * half, half), half), :])

        @pl.when(jnp.logical_and(outer, u >= 8))
        def _():
            i = u - 8
            for copy in link(3, i, to_pair):
                copy.wait_recv()
            put(i, q_recv[3, i], u_recv[3, i])

        @pl.when(jnp.logical_and(inner, jnp.logical_and(u >= 6, u < items + 6)))
        def _():
            i = u - 6
            far = received(2, i, to_middle)
            send(3, i, to_pair, decode(q_send[2, i], u_send[2, i]) + far)
            put(i, q_send[3, i], u_send[3, i])

        @pl.when(jnp.logical_and(inner, jnp.logical_and(u >= 4, u < items + 4)))
        def _():
            send(2, u - 4, to_middle, mine(u - 4)[...] + received(1, u - 4, to_pair))

        @pl.when(jnp.logical_and(u >= 2, u < items + 2))
        def _():
            total = mine(u - 2)[...] + received(0, u - 2, to_line)

            @pl.when(outer)
            def _():
                send(1, u - 2, to_pair, total)

            @pl.when(inner)
            def _():
                mine(u - 2)[...] = total

        @pl.when(u == items)
        def _():
            loading[c] = jnp.maximum(jnp.abs(flow_t[...] + high[...]), jnp.abs(flow_t[...] + low[...]))
            for d in range(1, n_cont):
                load_copy(c, lax.rem(c + d, n_cont)).start()

        return carry

    lax.fori_loop(0, items + 8, turn, 0)

    for d in range(1, n_cont):
        source = lax.rem(c + d, n_cont)
        load_copy(source, source).wait_recv()
    top = loading[0]
    for k in range(1, n_cont):
        top = jnp.maximum(top, loading[k])
    worst_ref[...] = top / lim_ref[...]

    for d in range(1, n_scen):
        meta_copy(q, lax.rem(q + d, n_scen)).wait_send()
    for d in range(1, n_cont):
        load_copy(c, lax.rem(c + d, n_cont)).wait_send()

    def drain(j, carry):
        for copy in link(0, j, to_line):
            copy.wait_send()

        @pl.when(outer)
        def _():
            for copy in link(1, j, to_pair):
                copy.wait_send()

        @pl.when(inner)
        def _():
            for copy in link(2, j, to_middle) + link(3, j, to_pair):
                copy.wait_send()

        return carry

    lax.fori_loop(0, items, drain, 0)


def fused(lodf, flow, out_flow, limits, ptdf_mon, ptdf_out, viol_cont, viol_line, viol_scen, rows_used):
    lines, conts = lodf.shape
    scens = flow.shape[1]
    width = ptdf_mon.shape[1]
    n_rows = viol_cont.shape[0]
    n_cont, n_line, n_scen = lax.axis_size("cont"), lax.axis_size("line"), lax.axis_size("scen")
    block = width // (n_line * n_scen)
    chunks = width // block
    half = block // 2
    items = 2 * chunks
    listed = n_scen * n_rows
    vmem = pl.BlockSpec(memory_space=pltpu.VMEM)
    dma = pltpu.SemaphoreType.DMA
    worst_t, code, unit = pl.pallas_call(
        functools.partial(kernel, (n_cont, n_line, n_scen)),
        out_shape=(
            jax.ShapeDtypeStruct((scens, lines), F32),
            jax.ShapeDtypeStruct((block, width), jnp.int16),
            jax.ShapeDtypeStruct((16, width), F32),
        ),
        in_specs=[vmem] * 10,
        out_specs=(vmem, vmem, vmem),
        scratch_shapes=[
            pltpu.VMEM((128, n_rows), F32),
            pltpu.VMEM((lines, conts), F32),
            pltpu.VMEM((scens, lines), F32),
            pltpu.VMEM((scens, lines), F32),
            pltpu.VMEM((n_cont, scens, lines), F32),
            pltpu.VMEM((listed, lines + conts), BF16),
            pltpu.VMEM((listed, 128), F32),
            pltpu.VMEM((2 * block, listed), BF16),
            pltpu.VMEM((n_line, listed, block), BF16),
            pltpu.VMEM((chunks, n_line * block, block), F32),
            pltpu.VMEM((4, items, half, block), jnp.int16),
            pltpu.VMEM((4, items, half, block), jnp.int16),
            pltpu.VMEM((4, items, 8, block), F32),
            pltpu.VMEM((4, items, 8, block), F32),
            dma((n_scen,)), dma((n_scen,)), dma((n_cont,)), dma((n_cont,)),
            dma((2, 4, items)), dma((2, 4, items)),
        ],
        compiler_params=pltpu.CompilerParams(collective_id=0, has_side_effects=True, vmem_limit_bytes=56 * 1024 * 1024),
    )(
        viol_line.reshape(1, n_rows), viol_cont.reshape(1, n_rows), viol_scen.reshape(1, n_rows),
        jnp.broadcast_to(rows_used, (1, 128)), limits.reshape(1, lines), lodf, flow.T, out_flow, ptdf_mon, ptdf_out,
    )
    root = code.astype(F32).reshape(2, half, width)
    unit = unit.reshape(2, 8, width)[:, 0:1, :] * (1.0 / (n_rows * n_cont * n_line * n_scen))
    return worst_t.T, (root * jnp.abs(root) * unit).reshape(block, width)


def local(
    lodf, flow, out_flow, limits, ptdf_mon, ptdf_out, viol_cont, viol_line, viol_scen, rows_used
):
    line_dev, cont_dev = lodf.shape
    scen_dev = flow.shape[1]
    width = ptdf_mon.shape[1]
    n_rows = viol_cont.shape[0]
    block = width // (lax.axis_size("line") * lax.axis_size("scen"))
    if (
        (lax.axis_size("cont"), lax.axis_size("line"), lax.axis_size("scen")) == (4, 2, 4)
        and line_dev == 128 and scen_dev <= 128 and scen_dev % 8 == 0
        and block % 256 == 0 and n_rows % 128 == 0 and cont_dev % 128 == 0
    ):
        return fused(
            lodf, flow, out_flow, limits, ptdf_mon, ptdf_out, viol_cont, viol_line, viol_scen, rows_used
        )
    n_cont = lax.axis_size("cont")
    n_line = lax.axis_size("line")
    n_scen = lax.axis_size("scen")
    owners = n_line * n_scen
    devices = n_cont * owners
    row_block = math.gcd(n_rows, 512)
    lines_each = math.gcd(line_dev, 32)

    def screen(pair):
        lodf_block, flow_block = pair
        post = (
            flow_block[:, :, None]
            + lodf_block.astype(jnp.float32)[:, None, :] * out_flow[None, :, :]
        )
        return jnp.max(jnp.abs(post), axis=2)

    local_worst = lax.map(
        screen,
        (
            lodf.reshape(line_dev // lines_each, lines_each, cont_dev),
            flow.reshape(line_dev // lines_each, lines_each, scen_dev),
        ),
    ).reshape(line_dev, scen_dev)
    worst = lax.pmax(local_worst, "cont") / limits[:, None]
    coef = lodf[viol_line, viol_cont].astype(jnp.float32)
    rows = (
        ptdf_mon[viol_line].astype(jnp.float32)
        + coef[:, None] * ptdf_out[viol_cont].astype(jnp.float32)
    ).astype(jnp.bfloat16)
    rows = lax.optimization_barrier(rows)
    post = flow[viol_line, viol_scen] + coef * out_flow[viol_scen, viol_cont]
    ratio = post / limits[viol_line]
    live = jnp.arange(n_rows, dtype=jnp.int32) < rows_used[0]
    weight = jnp.where(live, 1.0 + ratio * ratio, jnp.zeros_like(ratio))
    scaled = (weight[:, None] * rows.astype(jnp.float32)).astype(jnp.bfloat16)
    trips = (rows_used[0] + row_block - 1) // row_block
    row_blocks = rows.reshape(n_rows // row_block, row_block, width)
    scaled_blocks = scaled.reshape(n_rows // row_block, row_block, width)

    def step(index, acc):
        row_tile = lax.dynamic_index_in_dim(row_blocks, index, 0, keepdims=False)
        scaled_tile = lax.dynamic_index_in_dim(scaled_blocks, index, 0, keepdims=False)
        return acc + lax.dot_general(
            row_tile, scaled_tile, (((0,), (0,)), ((), ())), preferred_element_type=jnp.float32
        )

    owned = lax.psum_scatter(
        lax.fori_loop(
            0,
            trips,
            step,
            jnp.zeros((lax.axis_size(("line", "scen")) * (width // owners), width), jnp.float32),
        ),
        ("line", "scen"),
        scatter_dimension=0,
        tiled=True,
    )
    total = lax.psum(owned, "cont")
    schur = total * (1.0 / (n_rows * devices))
    return (worst, schur)


def solution(mesh):
    in_specs = (
        P("line", "cont"),
        P("line", "scen"),
        P("scen", "cont"),
        P("line"),
        P("line", None),
        P("cont", None),
        P(("cont", "line", "scen")),
        P(("cont", "line", "scen")),
        P(("cont", "line", "scen")),
        P(("cont", "line", "scen")),
    )
    out_specs = (P("line", "scen"), P(("line", "scen"), None))
    return jax.shard_map(local, mesh=mesh, in_specs=in_specs, out_specs=out_specs, check_vma=False)
```

profile of v0, /device:TPU:0, one launch (start us, length us, event | category | flops | bytes accessed | tf_op | source)
XLA Modules:
  0.0 74.1 jit_solution(577907736769021245)
XLA Ops:
  1.3 0.5 broadcast_in_dim.2.used_ref
  1.8 67.7 %shard_map.116 = (f32[64,128]{1,0:T(8,128)}, s16[256,2048]{1,0:T(8,128)(2,1)}, f32[16,2048]{1,0:T(8,128)}) custom-call(s32[1,512]{1,0:T(1,128)} %bitcast.17, s32[1,512]{1,0:T(1,128)} %bitcast.18, s32[1,512]{1,0:T(1,128)} %bitcast.19, s32[1,128]{1,0:T(1,128)} %broadcast_in_dim.2.used_ref, f32[1,128]{1,0:T(1,128)} %bitcast.21, bf16[128,1024]{1,0:T(8,128)(2,1)} %lodf_ref.1, ...), custom_call_target="tpu_custom_call" | custom-call | tf_op jit(solution)/shard_map/pallas_call | solution.py:300
  69.5 0.0 copy-start
  69.5 0.9 %slice_multiply_fusion = f32[2,1,2048]{2,1,0:T(1,128)S(1)} fusion(f32[2,8,2048]{2,1,0:T(8,128)} %bitcast.20), kind=kLoop, calls=%fused_computation.2 | loop fusion | flops 4096 | bytes 32768 | tf_op jit(solution)/shard_map/mul | solution.py:333
  70.5 3.0 %fusion = f32[256,2048]{1,0:T(8,128)} fusion(s16[256,2048]{1,0:T(8,128)(2,1)} %get-tuple-element.6, f32[2,2048]{1,0:T(2,128)S(1)} %bitcast.14), kind=kLoop, calls=%fused_computation.1 | loop fusion | flops 2097152 | bytes 3162112 | tf_op jit(solution)/shard_map/mul | solution.py:334
  73.5 0.0 copy-done
  73.5 0.6 copy.17
  (1 shorter events, 0.0 us)
Async XLA Ops:
  69.5 4.0 %copy-start = (f32[64,128]{1,0:T(8,128)S(1)}, f32[64,128]{1,0:T(8,128)}, u32[]{:S(2)}) copy-start(f32[64,128]{1,0:T(8,128)} %get-tuple-element.5) | copy-start | bytes 98308
where the time goes:
time: 74.3 us; the launch traced here: 74.1 us
  Pallas kernels  67.7 us (91%)
  other arithmetic  3.94 us (5%)
  between operations  1.3 us (2%)
  local copies, waits for them, and re-layouts  1.14 us (2%)
    pallas_call x1, Pallas kernels, fused(): pl.pallas_call(functools.partial(kernel, (n_cont, n_line, n_scen)), out_s...  67.7 us
    mul x1, other arithmetic, fused(): return (worst_t.T, (root * jnp.abs(root) * unit).reshape(block, width))  3.02 us

commit v1 on v0

--- a/solution.py
+++ b/solution.py
@@ -17,22 +17,33 @@
 
 def encode(x):
     top = jnp.maximum(jnp.max(jnp.abs(x), axis=0, keepdims=True), 1e-30)
-    unit = x * (1.0 / top)
+    power = jnp.ceil(jnp.log2(top) + 1e-3)
+    unit = x * jnp.exp2(-power)
     root = unit * lax.rsqrt(jnp.maximum(jnp.abs(unit), 1e-30)) * CODE
     code = jnp.round(root).astype(jnp.int32).astype(jnp.int16)
-    return code, jnp.broadcast_to(top * (1.0 / (CODE * CODE)), (8, x.shape[1]))
-
-
-def decode(code, unit):
+    power = jnp.broadcast_to(power, (16, x.shape[1])).astype(jnp.int32).astype(jnp.int16)
+    return code, power
+
+
+def decode(code, power, factor=1.0):
     root = code.astype(jnp.int32).astype(F32)
-    return root * jnp.abs(root) * unit[0:1, :]
+    unit = jnp.exp2(power.astype(jnp.int32).astype(F32)[0:1, :]) * (factor / (CODE * CODE))
+    return root * jnp.abs(root) * unit
+
+
+def finish(factor, worst_in, code_ref, power_ref, worst_ref, schur_ref):
+    worst_ref[...] = worst_in[...]
+    half = code_ref.shape[0] // 2
+    for h in range(2):
+        at = slice(h * half, (h + 1) * half)
+        schur_ref[at, :] = decode(code_ref[at, :], power_ref[h * 16:(h + 1) * 16, :], factor)
 
 
 def kernel(
     dims, line_ref, cont_ref, scen_ref, used_ref, lim_ref, lodf_ref, flow_t, out_flow_ref, mon_ref, out_ref,
-    worst_ref, code_ref, unit_ref,
+    worst_ref, code_ref, power_ref,
     meta, lodf32, high, low, loading, pick, weight, left, scaled, own,
-    q_send, q_recv, u_send, u_recv, meta_ss, meta_rs, load_ss, load_rs, send_sems, recv_sems,
+    q_send, q_recv, meta_ss, meta_rs, load_ss, load_rs, send_sems, recv_sems,
 ):
     n_cont, n_line, n_scen = dims
     c, m, q = lax.axis_index("cont"), lax.axis_index("line"), lax.axis_index("scen")
@@ -58,11 +69,10 @@
         pl.semaphore_signal(barrier, inc=1, device_id={"cont": lax.rem(c + d, n_cont)}, device_id_type=MESH)
     pl.semaphore_signal(barrier, inc=1, device_id={"line": other}, device_id_type=MESH)
 
-    meta[8 * n_scen:, :] = jnp.zeros((128 - 8 * n_scen, n_rows), F32)
     for p in range(parts):
         at = slice(p * 128, (p + 1) * 128)
         sub = lax.broadcasted_iota(jnp.int32, (128, 128), 0)
-        cols = jnp.where(sub == 0, line_ref[:, at], jnp.where(sub == 1, cont_ref[:, at], jnp.where(sub == 2, scen_ref[:, at], used_ref[...])))
+        cols = jnp.where(sub == 0, line_ref[:, at], jnp.where(sub == 1, cont_ref[:, at], jnp.where(sub == 2, scen_ref[:, at], used_ref[0])))
         cols = jnp.transpose(cols.astype(F32))
         v_line, v_cont, v_scen, used = cols[:, 0:1], cols[:, 1:2], cols[:, 2:3], cols[:, 3:4]
         lane = lax.broadcasted_iota(jnp.int32, (128, 128), 1)
@@ -97,15 +107,11 @@
     high[...] = jnp.zeros_like(high)
     low[...] = jnp.zeros_like(low)
 
-    for d in range(1, n_scen):
-        source = lax.rem(q + d, n_scen)
-        meta_copy(source, source).wait_recv()
-
-    for s in range(n_scen):
+    def pick_rows(s):
         for p in range(parts):
-            facts = jnp.transpose(meta[:, p * 128:(p + 1) * 128])
-            f = facts[:, s * 8:(s + 1) * 8]
-            at = slice(s * n_rows + p * 128, s * n_rows + (p + 1) * 128)
+            facts = meta[pl.ds(pl.multiple_of(s * 8, 8), 8), p * 128:(p + 1) * 128]
+            f = jnp.transpose(jnp.concatenate([facts, jnp.zeros((120, 128), F32)], axis=0))
+            at = pl.ds(pl.multiple_of(s * n_rows + p * 128, 128), 128)
             lane = lax.broadcasted_iota(jnp.int32, (128, lines), 1).astype(F32)
             pick[at, 0:lines] = jnp.where(lane == f[:, 0:1], 1.0, 0.0).astype(BF16)
             lane = lax.broadcasted_iota(jnp.int32, (128, conts), 1).astype(F32)
@@ -145,7 +151,14 @@
     def column(t):
         return (lax.rem(t, n_line) * n_scen + lax.rem(q + t // n_line, n_scen)) * block
 
-    def left_step(s, carry):
+    def left_step(d, carry):
+        s = lax.rem(q + d, n_scen)
+
+        @pl.when(d > 0)
+        def _():
+            meta_copy(s, s).wait_recv()
+
+        pick_rows(s)
         at = pl.ds(pl.multiple_of(s * n_rows, n_rows), n_rows)
         for line in range(n_line):
             rows = rows_of(s, column(line))
@@ -156,34 +169,31 @@
 
     lax.fori_loop(0, n_scen, left_step, 0)
 
-    def link(stage, j, to):
-        kinds = ((q_send, q_recv), (u_send, u_recv))
-        return [
-            pltpu.make_async_remote_copy(
-                src_ref=a.at[stage, j], dst_ref=b.at[stage, j], send_sem=send_sems.at[kind, stage, j],
-                recv_sem=recv_sems.at[kind, stage, j], device_id=to, device_id_type=MESH)
-            for kind, (a, b) in enumerate(kinds)
-        ]
+    def link(stage, i, to):
+        return pltpu.make_async_remote_copy(
+            src_ref=q_send.at[stage, i], dst_ref=q_recv.at[stage, i], send_sem=send_sems.at[stage, i],
+            recv_sem=recv_sems.at[stage, i], device_id=to, device_id_type=MESH)
 
     to_line, to_pair, to_middle = {"line": other}, {"cont": pair}, {"cont": middle}
 
-    def send(stage, j, to, value):
-        code, unit = encode(value)
-        q_send[stage, j] = code
-        u_send[stage, j] = unit
-        for copy in link(stage, j, to):
-            copy.start()
-
-    def received(stage, j, to):
-        for copy in link(stage, j, to):
-            copy.wait_recv()
-        return decode(q_recv[stage, j], u_recv[stage, j])
-
-    def put(i, code, unit):
+    def send(stage, i, to, value):
+        code, power = encode(value)
+        q_send[stage, i, 0:half] = code
+        q_send[stage, i, half:] = power
+        link(stage, i, to).start()
+
+    def value_of(ref, stage, i):
+        return decode(ref[stage, i, 0:half], ref[stage, i, half:])
+
+    def received(stage, i, to):
+        link(stage, i, to).wait_recv()
+        return value_of(q_recv, stage, i)
+
+    def put(ref, i):
         at = pl.ds(pl.multiple_of(lax.rem(i, 2) * half, half), half)
         cols = pl.ds(pl.multiple_of(column(i // 2), block), block)
-        code_ref[at, cols] = code
-        unit_ref[pl.ds(pl.multiple_of(lax.rem(i, 2) * 8, 8), 8), cols] = unit
+        code_ref[at, cols] = ref[3, i, 0:half]
+        power_ref[pl.ds(pl.multiple_of(lax.rem(i, 2) * 16, 16), 16), cols] = ref[3, i, half:]
 
     def mine(i):
         return own.at[i // 2, pl.ds(pl.multiple_of(m * block + lax.rem(i, 2) * half, half), half), :]
@@ -215,16 +225,15 @@
         @pl.when(jnp.logical_and(outer, u >= 8))
         def _():
             i = u - 8
-            for copy in link(3, i, to_pair):
-                copy.wait_recv()
-            put(i, q_recv[3, i], u_recv[3, i])
+            link(3, i, to_pair).wait_recv()
+            put(q_recv, i)
 
         @pl.when(jnp.logical_and(inner, jnp.logical_and(u >= 6, u < items + 6)))
         def _():
             i = u - 6
             far = received(2, i, to_middle)
-            send(3, i, to_pair, decode(q_send[2, i], u_send[2, i]) + far)
-            put(i, q_send[3, i], u_send[3, i])
+            send(3, i, to_pair, value_of(q_send, 2, i) + far)
+            put(q_send, i)
 
         @pl.when(jnp.logical_and(inner, jnp.logical_and(u >= 4, u < items + 4)))
         def _():
@@ -265,19 +274,17 @@
     for d in range(1, n_cont):
         load_copy(c, lax.rem(c + d, n_cont)).wait_send()
 
-    def drain(j, carry):
-        for copy in link(0, j, to_line):
-            copy.wait_send()
+    def drain(i, carry):
+        link(0, i, to_line).wait_send()
 
         @pl.when(outer)
         def _():
-            for copy in link(1, j, to_pair):
-                copy.wait_send()
+            link(1, i, to_pair).wait_send()
 
         @pl.when(inner)
         def _():
-            for copy in link(2, j, to_middle) + link(3, j, to_pair):
-                copy.wait_send()
+            link(2, i, to_middle).wait_send()
+            link(3, i, to_pair).wait_send()
 
         return carry
 
@@ -297,17 +304,17 @@
     listed = n_scen * n_rows
     vmem = pl.BlockSpec(memory_space=pltpu.VMEM)
     dma = pltpu.SemaphoreType.DMA
-    worst_t, code, unit = pl.pallas_call(
+    worst_t, code, power = pl.pallas_call(
         functools.partial(kernel, (n_cont, n_line, n_scen)),
         out_shape=(
             jax.ShapeDtypeStruct((scens, lines), F32),
             jax.ShapeDtypeStruct((block, width), jnp.int16),
-            jax.ShapeDtypeStruct((16, width), F32),
+            jax.ShapeDtypeStruct((32, width), jnp.int16),
         ),
-        in_specs=[vmem] * 10,
+        in_specs=[vmem] * 3 + [pl.BlockSpec(memory_space=pltpu.SMEM)] + [vmem] * 6,
         out_specs=(vmem, vmem, vmem),
         scratch_shapes=[
-            pltpu.VMEM((128, n_rows), F32),
+            pltpu.VMEM((8 * n_scen, n_rows), F32),
             pltpu.VMEM((lines, conts), F32),
             pltpu.VMEM((scens, lines), F32),
             pltpu.VMEM((scens, lines), F32),
@@ -317,21 +324,29 @@
             pltpu.VMEM((2 * block, listed), BF16),
             pltpu.VMEM((n_line, listed, block), BF16),
             pltpu.VMEM((chunks, n_line * block, block), F32),
-            pltpu.VMEM((4, items, half, block), jnp.int16),
-            pltpu.VMEM((4, items, half, block), jnp.int16),
-            pltpu.VMEM((4, items, 8, block), F32),
-            pltpu.VMEM((4, items, 8, block), F32),
+            pltpu.VMEM((4, items, half + 16, block), jnp.int16),
+            pltpu.VMEM((4, items, half + 16, block), jnp.int16),
             dma((n_scen,)), dma((n_scen,)), dma((n_cont,)), dma((n_cont,)),
-            dma((2, 4, items)), dma((2, 4, items)),
+            dma((4, items)), dma((4, items)),
         ],
         compiler_params=pltpu.CompilerParams(collective_id=0, has_side_effects=True, vmem_limit_bytes=56 * 1024 * 1024),
     )(
         viol_line.reshape(1, n_rows), viol_cont.reshape(1, n_rows), viol_scen.reshape(1, n_rows),
-        jnp.broadcast_to(rows_used, (1, 128)), limits.reshape(1, lines), lodf, flow.T, out_flow, ptdf_mon, ptdf_out,
+        rows_used, limits.reshape(1, lines), lodf, flow.T, out_flow, ptdf_mon, ptdf_out,
     )
-    root = code.astype(F32).reshape(2, half, width)
-    unit = unit.reshape(2, 8, width)[:, 0:1, :] * (1.0 / (n_rows * n_cont * n_line * n_scen))
-    return worst_t.T, (root * jnp.abs(root) * unit).reshape(block, width)
+    wide = 2 * block
+    worst_t, schur = pl.pallas_call(
+        functools.partial(finish, 1.0 / (n_rows * n_cont * n_line * n_scen)),
+        grid=(width // wide,),
+        out_shape=(jax.ShapeDtypeStruct((scens, lines), F32), jax.ShapeDtypeStruct((block, width), F32)),
+        in_specs=[
+            pl.BlockSpec((scens, lines), lambda i: (0, 0)),
+            pl.BlockSpec((block, wide), lambda i: (0, i)),
+            pl.BlockSpec((32, wide), lambda i: (0, i)),
+        ],
+        out_specs=(pl.BlockSpec((scens, lines), lambda i: (0, 0)), pl.BlockSpec((block, wide), lambda i: (0, i))),
+    )(worst_t, code, power)
+    return worst_t.T, schur
 
 
 def local(

time: 74.3 us -> 71.9 us (0.968)
  other arithmetic: 3.94 us -> 0 us
  Pallas kernels: 67.7 us -> 70.4 us
  local copies, waits for them, and re-layouts: 1.14 us -> 0 us
    mul x2 -> x0, other arithmetic: 3.94 us -> none  [the longest x1 3.02 us: fused(): return (worst_t.T, (root * jnp.abs(root) * unit).reshape(block, width))]
    pallas_call x0 -> x1, Pallas kernels: none -> 3.72 us  [fused(): pl.pallas_call(functools.partial(finish, 1.0 / (n_rows * n_cont * n_line...]
    pallas_call x1, Pallas kernels: 67.7 us -> 66.7 us  [fused(): pl.pallas_call(functools.partial(kernel, (n_cont, n_line, n_scen)), out_s...]
where the time goes in v1:
time: 71.9 us; the launch traced here: 71.7 us
  Pallas kernels  70.4 us (98%)
  between operations  1.29 us (2%)
    pallas_call x1, Pallas kernels, fused(): pl.pallas_call(functools.partial(kernel, (n_cont, n_line, n_scen)), out_s...  66.7 us
    pallas_call x1, Pallas kernels, fused(): pl.pallas_call(functools.partial(finish, 1.0 / (n_rows * n_cont * n_line...  3.72 us

profile of v1, /device:TPU:0, one launch (start us, length us, event | category | flops | bytes accessed | tf_op | source)
XLA Modules:
  0.0 71.7 jit_solution(13693805106653662032)
XLA Ops:
  1.3 66.7 %shard_map.113 = (f32[64,128]{1,0:T(8,128)}, s16[256,2048]{1,0:T(8,128)(2,1)}, s16[32,2048]{1,0:T(8,128)(2,1)}) custom-call(s32[1,512]{1,0:T(1,128)} %bitcast.7, s32[1,512]{1,0:T(1,128)} %bitcast.8, s32[1,512]{1,0:T(1,128)} %bitcast.9, s32[1]{0:T(128)S(6)} %copy.12.used_ref, f32[1,128]{1,0:T(1,128)} %bitcast.10, bf16[128,1024]{1,0:T(8,128)(2,1)} %lodf_ref.1, ...), custom_call_target="tpu_custom_call" | custom-call | tf_op jit(solution)/shard_map/pallas_call | solution.py:307
  68.0 3.7 %shard_map.114 = (f32[64,128]{1,0:T(8,128)}, f32[256,2048]{1,0:T(8,128)}) custom-call(f32[64,128]{1,0:T(8,128)} %get-tuple-element.7.worst_in, s16[256,2048]{1,0:T(8,128)(2,1)} %get-tuple-element.8.code_ref, s16[32,2048]{1,0:T(8,128)(2,1)} %get-tuple-element.9.power_ref), custom_call_target="tpu_custom_call" | custom-call | tf_op jit(solution)/shard_map/pallas_call | solution.py:338

commit v2 on v1

--- a/solution.py
+++ b/solution.py
@@ -118,8 +118,8 @@
             pick[at, lines:] = jnp.where(lane == f[:, 1:2], f[:, 2:3], 0.0).astype(BF16)
             weight[at, :] = jnp.broadcast_to(f[:, 3:4], (128, 128))
 
-    def rows_of(s, column):
-        at = pl.ds(pl.multiple_of(s * n_rows, n_rows), n_rows)
+    def rows_of(s, column, count):
+        at = pl.ds(pl.multiple_of(s * count, count), count)
         cols = pl.ds(pl.multiple_of(column, block), block)
         full = jnp.dot(pick[at, 0:lines], mon_ref[:, cols], preferred_element_type=F32)
         full = full + jnp.dot(pick[at, lines:], out_ref[:, cols], preferred_element_type=F32)
@@ -143,7 +143,8 @@
     lines_each = lines // (chunks * n_scen)
 
     def scale(s, slot, rows):
-        at = pl.ds(pl.multiple_of(s * n_rows, n_rows), n_rows)
+        count = rows.shape[0]
+        at = pl.ds(pl.multiple_of(s * count, count), count)
         w = weight[at, :]
         w = jnp.concatenate([w] * (block // 128), axis=1)
         scaled[slot, at, :] = (rows.astype(F32) * w).astype(BF16)
@@ -161,7 +162,7 @@
         pick_rows(s)
         at = pl.ds(pl.multiple_of(s * n_rows, n_rows), n_rows)
         for line in range(n_line):
-            rows = rows_of(s, column(line))
+            rows = rows_of(s, column(line), n_rows)
             left[line * block:(line + 1) * block, at] = jnp.transpose(rows.astype(F32)).astype(BF16)
             scale(s, line, rows)
         screen(s * n_line * lines_each, n_line * lines_each)
@@ -212,11 +213,11 @@
             @pl.when(t >= n_line)
             def _():
                 def scale_step(s, inside):
-                    scale(s, slot, rows_of(s, column(t)))
-                    screen((t * n_scen + s) * lines_each, lines_each)
+                    scale(s, slot, rows_of(s, column(t), 2 * n_rows))
+                    screen((t * n_scen + 2 * s) * lines_each, 2 * lines_each)
                     return inside
 
-                lax.fori_loop(0, n_scen, scale_step, 0)
+                lax.fori_loop(0, n_scen // 2, scale_step, 0)
 
             own[t] = jnp.dot(left[...], scaled[slot], preferred_element_type=F32)
             for h in range(2):

time: 71.9 us -> 71.1 us (0.989)
  Pallas kernels: 70.4 us -> 69.6 us
    pallas_call x1, Pallas kernels: 66.7 us -> 65.9 us  [fused(): pl.pallas_call(functools.partial(kernel, (n_cont, n_line, n_scen)), out_s...]
where the time goes in v2:
time: 71.1 us; the launch traced here: 70.9 us
  Pallas kernels  69.6 us (98%)
  between operations  1.29 us (2%)
    pallas_call x1, Pallas kernels, fused(): pl.pallas_call(functools.partial(kernel, (n_cont, n_line, n_scen)), out_s...  65.9 us
    pallas_call x1, Pallas kernels, fused(): pl.pallas_call(functools.partial(finish, 1.0 / (n_rows * n_cont * n_line...  3.72 us

profile of v2, /device:TPU:0, one launch (start us, length us, event | category | flops | bytes accessed | tf_op | source)
XLA Modules:
  0.0 70.9 jit_solution(17057762474774124250)
XLA Ops:
  1.3 65.9 %shard_map.113 = (f32[64,128]{1,0:T(8,128)}, s16[256,2048]{1,0:T(8,128)(2,1)}, s16[32,2048]{1,0:T(8,128)(2,1)}) custom-call(s32[1,512]{1,0:T(1,128)} %bitcast.7, s32[1,512]{1,0:T(1,128)} %bitcast.8, s32[1,512]{1,0:T(1,128)} %bitcast.9, s32[1]{0:T(128)S(6)} %copy.12.used_ref, f32[1,128]{1,0:T(1,128)} %bitcast.10, bf16[128,1024]{1,0:T(8,128)(2,1)} %lodf_ref.1, ...), custom_call_target="tpu_custom_call" | custom-call | tf_op jit(solution)/shard_map/pallas_call | solution.py:308
  67.2 3.7 %shard_map.114 = (f32[64,128]{1,0:T(8,128)}, f32[256,2048]{1,0:T(8,128)}) custom-call(f32[64,128]{1,0:T(8,128)} %get-tuple-element.7.worst_in, s16[256,2048]{1,0:T(8,128)(2,1)} %get-tuple-element.8.code_ref, s16[32,2048]{1,0:T(8,128)(2,1)} %get-tuple-element.9.power_ref), custom_call_target="tpu_custom_call" | custom-call | tf_op jit(solution)/shard_map/pallas_call | solution.py:339
